TPU v7x, 256 devices: a whole 4x4x8 slice. The times are simulated.
256 devices in a mesh: dp: 32 (over z_hi, x, core), tensor: 8 (over y, z_lo).
Axes of the slice: x: 4, y: 4, z: 8 (z_hi: 4, z_lo: 2; z = z_hi * 2 + z_lo), core: 2. Of those that a mesh axis runs over, the one named last changes fastest.
Arguments:
- hidden_in: bfloat16 [16384, 4608], P('dp'), may hold values from -6 to 6
- kv_weight: bfloat16 [4608, 4096], P(None, 'tensor'), may hold values from -0.09375 to 0.09375
- kv_cotangent: bfloat16 [16384, 4096], P('dp', 'tensor'), may hold values from -6 to 6
- token_counts: int32 [32], P('dp'), may hold values from 256 to 512, as said below
- block_signs: int32 [4096], P('tensor'), may hold values from 0 to 1
- level_table: float32 [256], replicated, may hold values from 0.4 to 2.5
- level_index: int32 [32, 4608], P('tensor'), may hold values from 0 to 255
Outputs:
- input_grad: bfloat16 [16384, 4608], P('dp', 'tensor')
- kv_grad: bfloat16 [4608, 4096], P(None, 'tensor')
Inputs may be any that keep to these rules, and one draw needn't show every extreme that they name: `token_counts`: slots of a replica at or beyond its count hold padding.
All inputs are finite; a program needn't handle non-finite values.
Results may differ from a plain program's by a relative error of at most 0.023.
Values may be sent and summed in bfloat16 or wider, within the bound.
A program may use at most 128 MiB of HBM per device.

v0:
```python
import math

import jax
import jax.numpy as jnp
from jax import lax
from jax.sharding import PartitionSpec as P

HEAD = 128


def sylvester(order):
    indices = jnp.arange(order, dtype=jnp.int32)
    common = jnp.bitwise_and(indices[:, None], indices[None, :])
    parity = jnp.zeros((order, order), jnp.int32)
    for bit_index in range(order.bit_length() - 1):
        parity = parity + jnp.bitwise_and(jnp.right_shift(common, bit_index), 1)
    return jnp.where(parity % 2 == 0, 1.0, -1.0).astype(jnp.float32)


def local(hidden_in, kv_weight, kv_cotangent, token_counts, block_signs, level_table, level_index):
    tok_rows = hidden_in.shape[0]
    model_width = hidden_in.shape[1]
    kv_cols = kv_weight.shape[1]
    block_count = kv_cols // HEAD
    valid_rows = jnp.arange(tok_rows, dtype=jnp.int32) < token_counts[0]
    masked = jnp.where(valid_rows[:, None], kv_cotangent, jnp.zeros_like(kv_cotangent))
    grad_rows = lax.psum_scatter(
        lax.dot_general(
            kv_weight, masked, (((1,), (1,)), ((), ())), preferred_element_type=jnp.float32
        ).astype(jnp.bfloat16),
        "tensor",
        scatter_dimension=0,
        tiled=True,
    ).astype(jnp.float32)
    input_grad = grad_rows.T.astype(jnp.bfloat16)
    sign_values = (2 * block_signs - 1).astype(jnp.float32)
    hadamard = sylvester(HEAD)
    hadamard_narrow = hadamard.astype(jnp.bfloat16)
    level_ids = jnp.arange(level_table.shape[0], dtype=jnp.int32)
    bounds = jnp.sum(jnp.where(level_index[..., None] == level_ids, level_table, 0.0), axis=-1).T
    replicas = lax.axis_size("dp")
    gradient = lax.dot_general(
        hidden_in, masked, (((0,), (0,)), ((), ())), preferred_element_type=jnp.float32
    ) / math.sqrt(tok_rows)
    rotated = jnp.einsum(
        "rjk,kl->rjl",
        (gradient * sign_values).reshape(
            model_width // replicas * lax.axis_size("dp"), block_count, HEAD
        ),
        hadamard,
        precision=lax.Precision.HIGHEST,
    ) / math.sqrt(HEAD)
    limits = bounds[..., None]
    summed = lax.psum_scatter(
        jnp.clip(rotated, -limits, limits)
        .reshape(model_width // replicas * lax.axis_size("dp"), kv_cols)
        .astype(jnp.bfloat16),
        "dp",
        scatter_dimension=0,
        tiled=True,
    ).astype(jnp.float32)
    requant = (summed / math.sqrt(replicas)).astype(jnp.bfloat16)
    blocks = lax.all_gather(requant, "dp", axis=0, tiled=True).reshape(-1, block_count, HEAD)
    rotated = jnp.einsum(
        "rjk,kl->rjl", blocks, hadamard_narrow, preferred_element_type=jnp.float32
    ) / math.sqrt(HEAD)
    kv_grad = (rotated.reshape(-1, kv_cols) * sign_values).astype(jnp.bfloat16)
    return (input_grad, kv_grad)


def solution(mesh):
    return jax.shard_map(
        local,
        mesh=mesh,
        in_specs=(
            P("dp", None),
            P(None, "tensor"),
            P("dp", "tensor"),
            P("dp"),
            P("tensor"),
            P(),
            P("tensor", None),
        ),
        out_specs=(P("dp", "tensor"), P(None, "tensor")),
        check_vma=False,
    )
```

profile of v0, /device:TPU:1, one launch (start us, length us, event | category | flops | bytes accessed | tf_op | source)
XLA Modules:
  0.0 291.1 jit_solution(10012499030504286461)
XLA Ops:
  8.0 0.0 reduce-scatter.9.cloned.1.call-start
  8.7 0.7 broadcast_multiply_fusion
  9.4 7.7 %select_reduce_fusion = f32[4,4608]{1,0:T(4,128)S(1)} fusion(f32[256]{0:T(256)} %param.12, s32[4,4608]{1,0:T(4,128)} %param.13), kind=kLoop, calls=%fused_computation | loop fusion | flops 14137344 | bytes 148480 | tf_op jit(solution)/shard_map/reduce_sum | solution.py:40
  17.1 4.9 %convolution_multiply_fusion.1 = f32[512,4608]{1,0:T(8,128)S(1)} fusion(bf16[512,4608]{1,0:T(8,128)(2,1)} %param.7, f32[512]{0:T(512)S(1)} %broadcast_multiply_fusion, bf16[512,512]{1,0:T(8,128)(2,1)} %param.9, pred[512]{0:T(512)(128)(4,1)S(1)} %iota_compare_fusion.1), kind=kOutput, calls=%fused_computation.5 | convolution fusion | flops 2418540544 | bytes 14682624 | tf_op jit(solution)/shard_map/dot_general | solution.py:42
  22.0 10.9 %minimum_convert_fusion = bf16[4608,4,128]{0,2,1:T(8,128)(2,1)} fusion(f32[4608,4,128]{0,2,1:T(8,128)S(1)} %bitcast.26, bf16[4608,4]{0,1:T(4,128)(2,1)S(1)} %bitcast_negate_fusion, f32[4608,4]{0,1:T(4,128)S(1)} %bitcast.30), kind=kOutput, calls=%fused_computation.3 | convolution fusion | flops 3638591488 | bytes 14266368 | tf_op jit(solution)/shard_map/rjk,kl->rjl/dot_general | solution.py:45
  32.9 0.0 copy-start
  32.9 6.7 %copy.38 = bf16[4608,512]{1,0:T(8,128)(2,1)} copy(bf16[4608,512]{0,1:T(8,128)(2,1)} %bitcast.28) | data formatting | bytes 9437184
  39.6 0.0 reduce-scatter.9.cloned.1.call-update
  39.6 0.0 all-gather.2.cloned.1.call-start
  39.7 105.0 %reduce-scatter.9.cloned.1.call-done = bf16[144,512]{1,0:T(8,128)(2,1)} async-done(((bf16[4608,512]{1,0:T(8,128)(2,1)}), bf16[144,512]{1,0:T(8,128)(2,1)}) %reduce-scatter.9.cloned.1.call-update) | async-done | bytes 147472 | tf_op jit(solution)/shard_map/reduce_scatter | solution.py:54
  144.7 1.6 multiply_convert_fusion.1
  146.3 0.0 all-gather.2.cloned.1.call-update
  146.3 0.0 reduce-scatter.7.cloned.1.call-start
  146.4 0.0 copy-done
  146.4 6.7 %fusion = bf16[4608,512]{0,1:T(8,128)(2,1)} fusion(bf16[4608,512]{1,0:T(8,128)(2,1)} %param.8, bf16[512,512]{1,0:T(8,128)(2,1)S(1)} %copy-done, pred[512]{0:T(512)(128)(4,1)S(1)} %iota_compare_fusion.1), kind=kOutput, calls=%fused_computation.7 | convolution fusion | flops 2418540544 | bytes 9961984 | tf_op jit(solution)/shard_map/dot_general | solution.py:28
  153.1 0.0 copy-start.1
  153.1 6.7 %copy.36 = bf16[4608,512]{1,0:T(8,128)(2,1)} copy(bf16[4608,512]{0,1:T(8,128)(2,1)} %fusion) | data formatting | bytes 9437184
  159.8 0.0 reduce-scatter.7.cloned.1.call-update
  159.8 0.0 copy-done.1
  159.8 93.0 %all-gather.2.cloned.1.call-done = bf16[4608,512]{1,0:T(8,128)(2,1)} async-done(((bf16[144,512]{1,0:T(8,128)(2,1)}), bf16[4608,512]{1,0:T(8,128)(2,1)}) %all-gather.2.cloned.1.call-update) | async-done | bytes 4718608 | tf_op jit(solution)/shard_map/all_gather | solution.py:63
  252.8 6.6 %copy.30 = bf16[4608,512]{0,1:T(8,128)(2,1)} copy(bf16[4608,512]{1,0:T(8,128)(2,1)} %all-gather.2.cloned.1.call-done) | data formatting | bytes 9437184 | tf_op jit(solution)/shard_map/all_gather | solution.py:63
  259.5 7.4 %convolution_multiply_fusion = f32[4608,4,128]{0,2,1:T(8,128)} fusion(bf16[4608,4,128]{0,2,1:T(8,128)(2,1)} %bitcast.29), kind=kOutput, calls=%fused_computation.4 | convolution fusion | flops 606912512 | bytes 14155776 | tf_op jit(solution)/shard_map/rjk,kl->rjl/dot_general | solution.py:64
  266.8 9.6 %copy.32 = f32[4608,512]{1,0:T(8,128)} copy(f32[4608,512]{0,1:T(8,128)} %bitcast.27) | data formatting | bytes 18874368 | tf_op jit(solution)/shard_map/reshape | solution.py:67
  276.4 7.3 %multiply_convert_fusion = bf16[4608,512]{1,0:T(8,128)(2,1)} fusion(f32[4608,512]{1,0:T(8,128)} %copy.32, f32[512]{0:T(512)S(1)} %add_convert_fusion), kind=kLoop, calls=%fused_computation.2 | loop fusion | flops 4718592 | bytes 14157824 | tf_op jit(solution)/shard_map/convert_element_type | solution.py:67
  283.7 0.0 reduce-scatter.7.cloned.1.call-done
  (3 shorter events, 0.0 us)
Async XLA Ops:
  8.0 136.7 %reduce-scatter.9.cloned.1.call-start = ((), (), s32[]{:S(2)}) async-start(), calls=%async_computation.4 | async-start | bytes 4866048 | tf_op jit(solution)/shard_map/reduce_scatter | solution.py:54
  32.9 113.5 %copy-start = (bf16[512,512]{1,0:T(8,128)(2,1)S(1)}, bf16[512,512]{1,0:T(8,128)(2,1)}, u32[]{:S(2)}) copy-start(bf16[512,512]{1,0:T(8,128)(2,1)} %param.9) | copy-start | bytes 1572868
  39.6 213.2 %all-gather.2.cloned.1.call-start = ((), (), s32[]{:S(2)}) async-start(), calls=%async_computation.2 | async-start | bytes 4866048 | tf_op jit(solution)/shard_map/all_gather | solution.py:63
  146.3 137.4 %reduce-scatter.7.cloned.1.call-start = ((), (), s32[]{:S(2)}) async-start(), calls=%async_computation.3 | async-start | bytes 5308416
  153.1 6.7 %copy-start.1 = (s32[512]{0:T(512)S(1)}, s32[512]{0:T(512)}, u32[]{:S(2)}) copy-start(s32[512]{0:T(512)} %param.11) | copy-start | bytes 6148
Sparse Core Ops, SparseCore 0:
  39.7 104.9 reduce-scatter.8
  147.6 105.2 all-gather.1
Sparse Core Ops, SparseCore 1:
  159.9 121.9 reduce-scatter.6
where the time goes:
time: 294 us; the launch traced here: 291 us
  waiting for transfers between devices  198 us (67%)
  matrix products  29.9 us (10%)
  local copies, waits for them, and re-layouts  29.6 us (10%)
  other arithmetic  17.3 us (6%)
  between operations  16.2 us (6%)
    reduce_scatter x1, waiting for transfers between devices, local(): lax.psum_scatter(jnp.clip(rotated, -limits, limits).reshape(model_width /...  105 us
    all_gather x1, waiting for transfers between devices, local(): lax.all_gather(requant, 'dp', axis=0, tiled=True)  93 us
    unnamed x6, local copies, waits for them, and re-layouts  13.4 us
    dot_general x1, matrix products, local(): jnp.einsum('rjk,kl->rjl', (gradient * sign_values).reshape(model_width //...  10.9 us
    reshape x1, local copies, waits for them, and re-layouts, local(): kv_grad = (rotated.reshape(-1, kv_cols) * sign_values).astype(jnp.bfloat16)  9.6 us
    reduce_sum x1, other arithmetic, local(): jnp.sum(jnp.where(level_index[..., None] == level_ids, level_table, 0.0),...  7.7 us
    dot_general x1, matrix products, local(): jnp.einsum('rjk,kl->rjl', blocks, hadamard_narrow, preferred_element_type...  7.39 us
    convert_element_type x1, other arithmetic, local(): kv_grad = (rotated.reshape(-1, kv_cols) * sign_values).astype(jnp.bfloat16)  7.25 us
  transfers between devices with their start and end apart: 3, of which 2 were waited for; matrix products, arithmetic and copies ran while one was open for 15% of the time, Pallas kernels for 0%

commit v1 on v0

v1 whole, which is shorter than its diff:
```python
import functools
import math

import jax
import jax.numpy as jnp
from jax import lax
from jax.experimental import pallas as pl
from jax.experimental.pallas import tpu as pltpu
from jax.sharding import PartitionSpec as P

MESH = pl.DeviceIdType.MESH
F32 = jnp.float32
BF16 = jnp.bfloat16
HEAD = 128
NX, NZ, NY = 4, 4, 4

KV_WAVES = (1, 2, 2, 2, 2)
Y_WAVES = (128, 128, 128, 128, 64)


def starts(sizes):
    out, at = [], 0
    for size in sizes:
        out.append(at)
        at += size
    return tuple(out)


KV_AT = starts(KV_WAVES)
Y_AT = starts(Y_WAVES)


def order():
    plan = []
    step = 4.6
    for w in range(len(KV_WAVES)):
        t = 0.0 if w == 0 else 2.0 + step * w
        for name, late in (
            ("encode", 0.0), ("pair", 3.0), ("x_mid", 6.5), ("x_end", 9.5), ("z_mid", 12.5), ("z_end", 15.5),
            ("z_pass", 18.5), ("x_own", 21.0), ("x_pass", 25.0), ("pair_last", 29.0),
        ):
            plan.append((t + late, name, w))
    step = 7.7
    for v in range(len(Y_WAVES)):
        t = 1.0 if v == 0 else 3.0 + step * v
        for name, late in (("partial", 0.0), ("y_mid", 5.0), ("y_end", 10.5), ("zl_end", 14.0)):
            plan.append((t + late, name, v))
    plan.sort()
    return [(name, w) for _, name, w in plan]


def rows_of(at, size):
    return pl.ds(pl.multiple_of(at, 16), size)


def add_rows(out, out_at, terms, size, block=32):
    block = min(block, size)

    def step(i, _):
        total = None
        for ref, at in terms:
            value = ref[rows_of(at + i * block, block), :].astype(F32)
            total = value if total is None else total + value
        out[rows_of(out_at + i * block, block), :] = total.astype(BF16)
        return 0

    lax.fori_loop(0, size // block, step, 0)


def kernel(
    count, hidden_hbm, weight_hbm, cot_hbm, signs_hbm, table_hbm, index_hbm,
    grad_out, input_out,
    hidden, weight, masked, signs, table, index, bt, enc, pair_in, summed,
    x_mid_in, x_in, x_sum, z_mid_in, z_in, part, y_mid_in, y_in, y_sum, zl_in,
    local_sem, send_sem, recv_sem,
):
    dp, tensor = lax.axis_index("dp"), lax.axis_index("tensor")
    zh, x, core = dp // 8, (dp // 2) % 4, dp % 2
    y, zl = tensor // 2, tensor % 2

    def dp_of(zh_, x_, core_):
        return ((zh_ % 4) * 4 + (x_ % 4)) * 2 + core_

    def at_dp(zh_, x_, core_):
        return (dp_of(zh_, x_, core_), tensor)

    peer = at_dp(zh, x, 1 - core)
    x_next, x_prev = at_dp(zh, x + 1, core), at_dp(zh, x + 3, core)
    z_next, z_prev = at_dp(zh + 1, x, core), at_dp(zh + 3, x, core)
    y_next, y_prev = (dp, ((y + 1) % 4) * 2 + zl), (dp, ((y + 3) % 4) * 2 + zl)
    zl_peer = (dp, y * 2 + 1 - zl)
    neighbours = (peer, x_next, x_prev, z_next, z_prev, y_next, y_prev, zl_peer)

    barrier = pltpu.get_barrier_semaphore()
    for device in neighbours:
        pl.semaphore_signal(barrier, inc=1, device_id=device, device_id_type=MESH)

    used = [0]
    local_used = [0]
    sent = []

    def load(src, dst):
        copy = pltpu.make_async_copy(src, dst, local_sem.at[local_used[0]])
        local_used[0] += 1
        copy.start()
        return copy

    def send(src, dst, device):
        copy = pltpu.make_async_remote_copy(
            src_ref=src, dst_ref=dst, send_sem=send_sem.at[used[0]], recv_sem=recv_sem.at[used[0]],
            device_id=device, device_id_type=MESH,
        )
        used[0] += 1
        copy.start()
        sent.append(copy)
        return copy

    cot_load = load(cot_hbm, masked)
    small_loads = [load(signs_hbm, signs), load(table_hbm, table), load(index_hbm, index)]
    hidden_loads, weight_loads = [], []

    def load_hidden(w):
        lanes = pl.ds(KV_AT[w] * 512, KV_WAVES[w] * 512)
        hidden_loads.append(load(hidden_hbm.at[:, lanes], hidden.at[:, lanes]))

    def load_weight(v):
        size = Y_WAVES[v]
        weight_loads.append([
            load(weight_hbm.at[pl.ds(t * 576 + Y_AT[v], size), :], weight.at[pl.ds(8 * Y_AT[v] + t * size, size), :])
            for t in range(8)
        ])

    for w in range(max(len(KV_WAVES), len(Y_WAVES))):
        if w < len(KV_WAVES):
            load_hidden(w)
        if w < len(Y_WAVES):
            load_weight(w)

    row_i = lax.broadcasted_iota(jnp.int32, (HEAD, HEAD), 0)
    col_i = lax.broadcasted_iota(jnp.int32, (HEAD, HEAD), 1)
    common = row_i & col_i
    common = common ^ (common >> 4)
    common = common ^ (common >> 2)
    common = common ^ (common >> 1)
    hadamard = (1 - 2 * (common & 1)).astype(F32)

    cot_load.wait()
    tokens = lax.broadcasted_iota(jnp.int32, (512, 512), 0)
    masked[...] = jnp.where(tokens < count[0], masked[...].astype(F32), 0.0).astype(BF16)
    for copy in small_loads:
        copy.wait()
    sign_row = (2 * signs[...] - 1).astype(F32)
    for j in range(4):
        lanes = pl.ds(j * HEAD, HEAD)
        turned = (hadamard * sign_row[:, j * HEAD:(j + 1) * HEAD]).astype(BF16)
        bt[lanes, :] = (
            lax.dot_general(turned, masked[:, lanes], (((1,), (1,)), ((), ())), preferred_element_type=F32)
            * (1.0 / 256.0)
        ).astype(BF16)

    waiting = {}

    def encode(w):
        hidden_loads[w].wait()

        def tile(i, _):
            at = pl.multiple_of((KV_AT[w] + i) * 512, 512)
            value = jnp.dot(bt[...], hidden[:, pl.ds(at, 512)], preferred_element_type=F32)
            low = jnp.broadcast_to(table[:, 0:128], (4, 128))
            high = jnp.broadcast_to(table[:, 128:256], (4, 128))
            bounds = []
            for k in range(4):
                ids = index[:, pl.ds(at + k * 128, 128)]
                first = jnp.take_along_axis(low, ids & 127, axis=1, mode="promise_in_bounds")
                second = jnp.take_along_axis(high, ids & 127, axis=1, mode="promise_in_bounds")
                bounds.append(jnp.where(ids >= 128, second, first))
            bound = jnp.concatenate(bounds, axis=1)
            for j in range(4):
                limit = bound[j:j + 1, :]
                clipped = jnp.clip(value[j * HEAD:(j + 1) * HEAD], -limit, limit).astype(BF16)
                enc[pl.ds(at, 512), pl.ds(j * HEAD, HEAD)] = clipped.T
            return 0

        lax.fori_loop(0, KV_WAVES[w], tile, 0)

    def own_rows(w, core_):
        g = KV_WAVES[w]
        return KV_AT[w] * 512 + core_ * 256 * g, 256 * g

    def pair_send(w):
        at, size = own_rows(w, 1 - core)
        waiting["pair", w] = send(
            enc.at[rows_of(at, size), :], pair_in.at[pl.ds(KV_AT[w] * 256, size), :], peer
        )

    class Axis:
        def __init__(self, name, place, following, previous, source, mid_in, into, half, by_lanes):
            self.name, self.place, self.next, self.prev = name, place, following, previous
            self.source, self.mid_in, self.into = source, mid_in, into
            self.half, self.by_lanes = half, by_lanes

        def piece(self, ref, base, chunk, half, h):
            if self.by_lanes:
                return ref.at[rows_of(base + chunk * half, half), pl.ds(h * 256, 256)]
            return ref.at[rows_of(base + chunk * 2 * half + h * half, half), :]

        def begin(self, w, base, half, at):
            mid_at = at if self.by_lanes else at // 2
            mid_rows = pl.ds(mid_at, half)
            here = functools.partial(self.piece, self.source, base)
            far, up, down = (self.place + 2) % 4, (self.place + 1) % 4, (self.place + 3) % 4
            a_up = send(here(far, half, 0), self.mid_in.at[0, mid_rows], self.next)
            a_down = send(here(far, half, 1), self.mid_in.at[1, mid_rows], self.prev)
            b_up = send(here(up, half, 1), self.piece(self.into.at[0], at, 0, half, 1), self.next)
            b_down = send(here(down, half, 0), self.piece(self.into.at[1], at, 0, half, 0), self.prev)
            waiting[self.name, w] = (a_up, a_down, b_up, b_down)

        def middle(self, w, base, half, at):
            mid_at = at if self.by_lanes else at // 2
            a_up, a_down, b_up, b_down = waiting.pop((self.name, w))
            up, down = (self.place + 1) % 4, (self.place + 3) % 4
            sends = []
            for h, chunk, copy, device in ((0, up, a_up, self.next), (1, down, a_down, self.prev)):
                copy.wait_recv()
                if self.by_lanes:
                    rows, lanes = rows_of(base + chunk * half, half), pl.ds(h * 256, 256)
                    self.source[rows, lanes] = (
                        self.source[rows, lanes].astype(F32) + self.mid_in[h, pl.ds(mid_at, half)].astype(F32)
                    ).astype(BF16)
                else:
                    first = base + chunk * 2 * half + h * half
                    add_rows(self.source, first, ((self.source, first), (self.mid_in.at[h], mid_at)), half)
                sends.append(send(
                    self.piece(self.source, base, chunk, half, h), self.piece(self.into.at[h], at, 0, half, h), device
                ))
            waiting[self.name, w] = (b_up, b_down, *sends)

        def arrive(self, w):
            for copy in waiting.pop((self.name, w)):
                copy.wait_recv()

    x_axis = Axis("x", x, x_next, x_prev, summed, x_mid_in, x_in, None, False)
    z_axis = Axis("z", zh, z_next, z_prev, x_sum, z_mid_in, z_in, None, True)
    y_axis = Axis("y", y, y_next, y_prev, part, y_mid_in, y_in, None, False)

    def x_args(w):
        g = KV_WAVES[w]
        return KV_AT[w] * 256, 32 * g, KV_AT[w] * 64

    def z_args(w):
        g = KV_WAVES[w]
        return KV_AT[w] * 64, 16 * g, KV_AT[w] * 16

    def y_args(v):
        return 8 * Y_AT[v], Y_WAVES[v], 2 * Y_AT[v]

    def chunk_row(w, x_, zh_=None):
        g = KV_WAVES[w]
        row = KV_AT[w] * 512 + core * 256 * g + (x_ % 4) * 64 * g
        return row if zh_ is None else row + (zh_ % 4) * 16 * g

    def do_pair(w):
        waiting.pop(("pair", w)).wait_recv()
        at, size = own_rows(w, core)
        add_rows(summed, KV_AT[w] * 256, ((enc, at), (pair_in, KV_AT[w] * 256)), size)
        x_axis.begin(w, *x_args(w))

    def do_x_end(w):
        x_axis.arrive(w)
        base, half, at = x_args(w)
        add_rows(
            x_sum, at, ((summed, base + x * 2 * half), (x_in.at[0], at), (x_in.at[1], at)), 2 * half
        )
        z_axis.begin(w, *z_args(w))

    def do_z_end(w):
        z_axis.arrive(w)
        base, half, at = z_args(w)
        rows = pl.ds(at, half)
        total = (
            x_sum[rows_of(base + zh * half, half), :].astype(F32) + z_in[0, rows].astype(F32) + z_in[1, rows].astype(F32)
        )
        requant = (total * (1.0 / math.sqrt(32.0))).astype(BF16)
        row = chunk_row(w, x, zh)
        for j in range(4):
            lanes = slice(j * HEAD, (j + 1) * HEAD)
            decoded = jnp.dot(requant[:, lanes], hadamard.astype(BF16), preferred_element_type=F32)
            grad_out[rows_of(row, half), lanes] = (
                decoded * (1.0 / math.sqrt(HEAD)) * sign_row[:, lanes]
            ).astype(BF16)
        whole = grad_out.at[rows_of(row, half), :]
        waiting["zg", w] = (send(whole, whole, z_next), send(whole, whole, z_prev))

    def do_z_pass(w):
        up, down = waiting.pop(("zg", w))
        half = 16 * KV_WAVES[w]
        up.wait_recv()
        piece = grad_out.at[rows_of(chunk_row(w, x, zh + 3), half), pl.ds(0, 256)]
        first = send(piece, piece, z_next)
        down.wait_recv()
        piece = grad_out.at[rows_of(chunk_row(w, x, zh + 1), half), pl.ds(256, 256)]
        second = send(piece, piece, z_prev)
        waiting["zg", w] = (first, second)

    def do_x_own(w):
        for copy in waiting.pop(("zg", w)):
            copy.wait_recv()
        whole = grad_out.at[rows_of(chunk_row(w, x), 64 * KV_WAVES[w]), :]
        waiting["xg", w] = (send(whole, whole, x_next), send(whole, whole, x_prev))
        waiting["pg", w] = [send(whole, whole, peer)]

    def do_x_pass(w):
        up, down = waiting.pop(("xg", w))
        half = 32 * KV_WAVES[w]
        up.wait_recv()
        piece = grad_out.at[rows_of(chunk_row(w, x + 3), half), :]
        first = send(piece, piece, x_next)
        whole = grad_out.at[rows_of(chunk_row(w, x + 3), 2 * half), :]
        waiting["pg", w].append(send(whole, whole, peer))
        down.wait_recv()
        piece = grad_out.at[rows_of(chunk_row(w, x + 1) + half, half), :]
        second = send(piece, piece, x_prev)
        whole = grad_out.at[rows_of(chunk_row(w, x + 1), 2 * half), :]
        waiting["pg", w].append(send(whole, whole, peer))
        waiting["xg", w] = (first, second)

    def do_pair_last(w):
        for copy in waiting.pop(("xg", w)):
            copy.wait_recv()
        whole = grad_out.at[rows_of(chunk_row(w, x + 2), 64 * KV_WAVES[w]), :]
        waiting["pg", w].append(send(whole, whole, peer))

    def partial(v):
        for copy in weight_loads[v]:
            copy.wait()
        tile_rows = 512

        def tile(i, _):
            rows = rows_of(8 * Y_AT[v] + i * tile_rows, tile_rows)
            part[rows, :] = lax.dot_general(
                weight[rows, :], masked[...], (((1,), (1,)), ((), ())), preferred_element_type=F32
            ).astype(BF16)
            return 0

        lax.fori_loop(0, 8 * Y_WAVES[v] // tile_rows, tile, 0)

    def do_y_end(v):
        y_axis.arrive(v)
        base, half, at = y_args(v)
        add_rows(y_sum, at, ((part, base + y * 2 * half), (y_in.at[0], at), (y_in.at[1], at)), 2 * half)
        waiting["zl", v] = send(
            y_sum.at[rows_of(at + (1 - zl) * half, half), :], zl_in.at[pl.ds(Y_AT[v], half), :], zl_peer
        )

    def do_zl_end(v):
        waiting.pop(("zl", v)).wait_recv()
        base, half, at = y_args(v)
        total = (
            y_sum[rows_of(at + zl * half, half), :].astype(F32) + zl_in[pl.ds(Y_AT[v], half), :].astype(F32)
        ).astype(BF16)
        input_out[pl.ds(Y_AT[v], half), :] = total

    met = False
    for name, w in order():
        if name == "encode":
            encode(w)
            if not met:
                pl.semaphore_wait(barrier, len(neighbours))
                met = True
            pair_send(w)
        elif name == "pair":
            do_pair(w)
        elif name == "x_mid":
            x_axis.middle(w, *x_args(w))
        elif name == "x_end":
            do_x_end(w)
        elif name == "z_mid":
            z_axis.middle(w, *z_args(w))
        elif name == "z_end":
            do_z_end(w)
        elif name == "z_pass":
            do_z_pass(w)
        elif name == "x_own":
            do_x_own(w)
        elif name == "x_pass":
            do_x_pass(w)
        elif name == "pair_last":
            do_pair_last(w)
        elif name == "partial":
            partial(w)
            y_axis.begin(w, *y_args(w))
        elif name == "y_mid":
            y_axis.middle(w, *y_args(w))
        elif name == "y_end":
            do_y_end(w)
        elif name == "zl_end":
            do_zl_end(w)

    for w in range(len(KV_WAVES)):
        for copy in waiting.pop(("pg", w)):
            copy.wait_recv()
    for copy in sent:
        copy.wait_send()


def local(hidden_in, kv_weight, kv_cotangent, token_counts, block_signs, level_table, level_index):
    hbm = pl.BlockSpec(memory_space=pltpu.HBM)
    vmem = pl.BlockSpec(memory_space=pltpu.VMEM)
    grad, input_t = pl.pallas_call(
        kernel,
        out_shape=(
            jax.ShapeDtypeStruct((4608, 512), BF16),
            jax.ShapeDtypeStruct((576, 512), BF16),
        ),
        in_specs=[pl.BlockSpec(memory_space=pltpu.SMEM)] + [hbm] * 6,
        out_specs=(vmem, vmem),
        scratch_shapes=[
            pltpu.VMEM((512, 4608), BF16),
            pltpu.VMEM((4608, 512), BF16),
            pltpu.VMEM((512, 512), BF16),
            pltpu.VMEM((1, 512), jnp.int32),
            pltpu.VMEM((1, 256), F32),
            pltpu.VMEM((4, 4608), jnp.int32),
            pltpu.VMEM((512, 512), BF16),
            pltpu.VMEM((4608, 512), BF16),
            pltpu.VMEM((2304, 512), BF16),
            pltpu.VMEM((2304, 512), BF16),
            pltpu.VMEM((2, 288, 512), BF16),
            pltpu.VMEM((2, 576, 512), BF16),
            pltpu.VMEM((576, 512), BF16),
            pltpu.VMEM((2, 144, 256), BF16),
            pltpu.VMEM((2, 144, 512), BF16),
            pltpu.VMEM((4608, 512), BF16),
            pltpu.VMEM((2, 576, 512), BF16),
            pltpu.VMEM((2, 1152, 512), BF16),
            pltpu.VMEM((1152, 512), BF16),
            pltpu.VMEM((576, 512), BF16),
            pltpu.SemaphoreType.DMA((64,)),
            pltpu.SemaphoreType.DMA((192,)),
            pltpu.SemaphoreType.DMA((192,)),
        ],
        compiler_params=pltpu.CompilerParams(
            collective_id=0, has_side_effects=True, vmem_limit_bytes=48 * 2**20
        ),
        cost_estimate=pl.CostEstimate(flops=5 * 10**9, bytes_accessed=15 * 10**6, transcendentals=0),
        name="reduce_both",
    )(
        token_counts, hidden_in, kv_weight, kv_cotangent, block_signs.reshape(1, 512), level_table.reshape(1, 256),
        level_index,
    )
    return input_t.T, grad


def solution(mesh):
    return jax.shard_map(
        local,
        mesh=mesh,
        in_specs=(
            P("dp", None),
            P(None, "tensor"),
            P("dp", "tensor"),
            P("dp"),
            P("tensor"),
            P(),
            P("tensor", None),
        ),
        out_specs=(P("dp", "tensor"), P(None, "tensor")),
        check_vma=False,
    )
```

time: 294 us -> 88 us (0.30)
  waiting for transfers between devices: 198 us -> 0 us
  Pallas kernels: 0 us -> 80.2 us
  matrix products: 29.9 us -> 0 us
  local copies, waits for them, and re-layouts: 29.6 us -> 6.28 us
  other arithmetic: 17.3 us -> 0 us
  between operations: 16.2 us -> 1.3 us
    reduce_scatter x1 -> x0, waiting for transfers between devices: 105 us -> none  [local(): lax.psum_scatter(jnp.clip(rotated, -limits, limits).reshape(model_width /...]
    all_gather x1 -> x0, waiting for transfers between devices: 93 us -> none  [local(): lax.all_gather(requant, 'dp', axis=0, tiled=True)]
    pallas_call x0 -> x1, Pallas kernels: none -> 80.2 us  [local(): pl.pallas_call(kernel, out_shape=(jax.ShapeDtypeStruct((4608, 512), BF16)...]
    dot_general x4 -> x0, matrix products: 29.9 us -> none  [the longest x1 10.9 us: local(): jnp.einsum('rjk,kl->rjl', (gradient * sign_values).reshape(model_width //...]
    reshape x1 -> x0, local copies, waits for them, and re-layouts: 9.6 us -> none  [local(): kv_grad = (rotated.reshape(-1, kv_cols) * sign_values).astype(jnp.bfloat16)]
    convert_element_type x3 -> x0, other arithmetic: 8.85 us -> none  [the longest x1 7.25 us: local(): kv_grad = (rotated.reshape(-1, kv_cols) * sign_values).astype(jnp.bfloat16)]
    reduce_sum x1 -> x0, other arithmetic: 7.7 us -> none  [local(): jnp.sum(jnp.where(level_index[..., None] == level_ids, level_table, 0.0),...]
    unnamed x6 -> x10, local copies, waits for them, and re-layouts: 13.4 us -> 6.28 us
  transfers between devices with their start and end apart: 3 -> 0, of which waited for: 2 -> 0; matrix products, arithmetic and copies ran while one was open for 15% -> 0% of each run, Pallas kernels for 0% -> 0%
where the time goes in v1:
time: 88 us; the launch traced here: 87.8 us
  Pallas kernels  80.2 us (91%)
  local copies, waits for them, and re-layouts  6.28 us (7%)
  between operations  1.3 us (1%)
    pallas_call x1, Pallas kernels, local(): pl.pallas_call(kernel, out_shape=(jax.ShapeDtypeStruct((4608, 512), BF16)...  80.2 us
    unnamed x10, local copies, waits for them, and re-layouts  6.28 us

profile of v1, /device:TPU:1, one launch (start us, length us, event | category | flops | bytes accessed | tf_op | source)
XLA Modules:
  0.0 87.8 jit_solution(9590374206967886094)
XLA Ops:
  1.3 0.0 copy-start
  1.3 1.0 %copy-done = bf16[512,512]{1,0:T(8,128)(2,1)S(1)} copy-done((bf16[512,512]{1,0:T(8,128)(2,1)S(1)}, bf16[512,512]{1,0:T(8,128)(2,1)}, u32[]{:S(2)}) %copy-start) | copy-done | bytes 524312
  2.3 0.0 copy-start.1
  2.3 0.9 %copy-done.1 = s32[4,4608]{1,0:T(4,128)S(1)} copy-done((s32[4,4608]{1,0:T(4,128)S(1)}, s32[4,4608]{1,0:T(4,128)}, u32[]{:S(2)}) %copy-start.1) | copy-done | bytes 73752
  3.2 0.0 copy-start.2
  3.2 0.7 copy-done.2
  3.9 0.0 copy-start.3
  3.9 0.7 copy-done.3
  4.6 80.2 %reduce_both.1 = (bf16[4608,512]{1,0:T(8,128)(2,1)S(1)}, bf16[576,512]{1,0:T(8,128)(2,1)S(1)}) custom-call(s32[1]{0:T(128)S(6)} %copy.11.count, bf16[512,4608]{1,0:T(8,128)(2,1)} %hidden_hbm.1, bf16[4608,512]{1,0:T(8,128)(2,1)} %weight_hbm.1, bf16[512,512]{1,0:T(8,128)(2,1)S(1)} %copy-done, s32[1,512]{1,0:T(1,128)S(1)} %bitcast.4, f32[1,256]{1,0:T(1,128)S(1)} %bitcast.5, ...), custom_call_target="tpu_custom_call" | custom-call | flops 5000000000 | bytes 15000000 | tf_op jit(solution)/shard_map/reduce_both/pallas_call | solution.py:409
  84.8 0.8 copy.12
  85.6 2.2 %copy.13 = bf16[4608,512]{1,0:T(8,128)(2,1)} copy(bf16[4608,512]{1,0:T(8,128)(2,1)S(1)} %get-tuple-element.9) | data formatting | bytes 9437184
Async XLA Ops:
  1.3 1.0 %copy-start = (bf16[512,512]{1,0:T(8,128)(2,1)S(1)}, bf16[512,512]{1,0:T(8,128)(2,1)}, u32[]{:S(2)}) copy-start(bf16[512,512]{1,0:T(8,128)(2,1)} %cot_hbm.1) | copy-start | bytes 1572868
  2.3 0.9 %copy-start.1 = (s32[4,4608]{1,0:T(4,128)S(1)}, s32[4,4608]{1,0:T(4,128)}, u32[]{:S(2)}) copy-start(s32[4,4608]{1,0:T(4,128)} %index_hbm.1) | copy-start | bytes 221188
  3.2 0.7 copy-start.2
  3.9 0.7 copy-start.3

commit v2 on v1

--- a/solution.py
+++ b/solution.py
@@ -14,8 +14,8 @@
 HEAD = 128
 NX, NZ, NY = 4, 4, 4
 
-KV_WAVES = (1, 2, 2, 2, 2)
-Y_WAVES = (128, 128, 128, 128, 64)
+KV_WAVES = (1, 1, 1, 1, 1, 1, 1, 1, 1)
+Y_WAVES = (64, 128, 128, 128, 128)
 
 
 def starts(sizes):
@@ -30,23 +30,24 @@
 Y_AT = starts(Y_WAVES)
 
 
-def order():
-    plan = []
-    step = 4.6
-    for w in range(len(KV_WAVES)):
-        t = 0.0 if w == 0 else 2.0 + step * w
-        for name, late in (
-            ("encode", 0.0), ("pair", 3.0), ("x_mid", 6.5), ("x_end", 9.5), ("z_mid", 12.5), ("z_end", 15.5),
-            ("z_pass", 18.5), ("x_own", 21.0), ("x_pass", 25.0), ("pair_last", 29.0),
-        ):
-            plan.append((t + late, name, w))
-    step = 7.7
-    for v in range(len(Y_WAVES)):
-        t = 1.0 if v == 0 else 3.0 + step * v
-        for name, late in (("partial", 0.0), ("y_mid", 5.0), ("y_end", 10.5), ("zl_end", 14.0)):
-            plan.append((t + late, name, v))
-    plan.sort()
-    return [(name, w) for _, name, w in plan]
+ORDER = (
+    ("encode", 0), ("encode", 1), ("partial", 0), ("encode", 2), ("encode", 3), ("encode", 4), ("pair", 1),
+    ("pair", 2), ("pair", 3), ("encode", 5), ("encode", 6), ("encode", 7), ("x_mid", 1), ("y_mid", 0),
+    ("x_mid", 2), ("pair", 0), ("pair", 5), ("partial", 1), ("x_end", 1), ("x_mid", 3), ("partial", 2),
+    ("x_end", 2), ("pair", 7), ("encode", 8), ("y_end", 0), ("x_mid", 5), ("x_mid", 0), ("partial", 3),
+    ("z_mid", 1), ("x_mid", 7), ("z_mid", 2), ("x_end", 3), ("pair", 8), ("pair", 4), ("x_end", 5),
+    ("x_end", 0), ("z_end", 1), ("x_end", 7), ("z_end", 2), ("x_mid", 8), ("z_mid", 3), ("x_mid", 4),
+    ("z_mid", 5), ("zl_end", 0), ("y_mid", 2), ("z_mid", 0), ("pair", 6), ("z_pass", 1), ("x_end", 8),
+    ("z_mid", 7), ("x_end", 4), ("y_mid", 1), ("z_pass", 2), ("z_end", 3), ("x_mid", 6), ("z_end", 5),
+    ("z_end", 0), ("z_mid", 8), ("y_mid", 3), ("z_mid", 4), ("x_own", 1), ("x_end", 6), ("z_pass", 3),
+    ("z_end", 7), ("x_own", 2), ("z_pass", 5), ("z_pass", 0), ("z_end", 8), ("x_pass", 1), ("z_mid", 6),
+    ("z_end", 4), ("x_own", 3), ("partial", 4), ("x_own", 5), ("z_pass", 7), ("z_pass", 8), ("x_pass", 2),
+    ("z_end", 6), ("pair_last", 1), ("x_own", 0), ("z_pass", 4), ("y_end", 2), ("x_own", 7), ("x_own", 8),
+    ("z_pass", 6), ("pair_last", 2), ("x_pass", 0), ("x_pass", 5), ("y_end", 3), ("y_end", 1), ("y_mid", 4),
+    ("x_pass", 3), ("x_own", 4), ("x_own", 6), ("x_pass", 8), ("pair_last", 0), ("pair_last", 3), ("zl_end", 2),
+    ("pair_last", 5), ("x_pass", 7), ("x_pass", 4), ("y_end", 4), ("x_pass", 6), ("pair_last", 7),
+    ("pair_last", 4), ("pair_last", 8), ("pair_last", 6), ("zl_end", 1), ("zl_end", 3), ("zl_end", 4),
+)
 
 
 def rows_of(at, size):
@@ -91,10 +92,6 @@
     zl_peer = (dp, y * 2 + 1 - zl)
     neighbours = (peer, x_next, x_prev, z_next, z_prev, y_next, y_prev, zl_peer)
 
-    barrier = pltpu.get_barrier_semaphore()
-    for device in neighbours:
-        pl.semaphore_signal(barrier, inc=1, device_id=device, device_id_type=MESH)
-
     used = [0]
     local_used = [0]
     sent = []
@@ -119,22 +116,29 @@
     small_loads = [load(signs_hbm, signs), load(table_hbm, table), load(index_hbm, index)]
     hidden_loads, weight_loads = [], []
 
-    def load_hidden(w):
-        lanes = pl.ds(KV_AT[w] * 512, KV_WAVES[w] * 512)
-        hidden_loads.append(load(hidden_hbm.at[:, lanes], hidden.at[:, lanes]))
+    def load_hidden(first, last):
+        lanes = pl.ds(KV_AT[first] * 512, sum(KV_WAVES[first:last]) * 512)
+        copy = load(hidden_hbm.at[:, lanes], hidden.at[:, lanes])
+        hidden_loads.extend([copy] + [None] * (last - first - 1))
 
     def load_weight(v):
-        size = Y_WAVES[v]
-        weight_loads.append([
-            load(weight_hbm.at[pl.ds(t * 576 + Y_AT[v], size), :], weight.at[pl.ds(8 * Y_AT[v] + t * size, size), :])
-            for t in range(8)
-        ])
-
-    for w in range(max(len(KV_WAVES), len(Y_WAVES))):
-        if w < len(KV_WAVES):
-            load_hidden(w)
-        if w < len(Y_WAVES):
-            load_weight(w)
+        rows = pl.ds(Y_AT[v], Y_WAVES[v])
+        weight_loads.append(load(weight_hbm.at[:, rows, :], weight.at[:, rows, :]))
+
+    load_hidden(0, 1)
+    barrier = pltpu.get_barrier_semaphore()
+    for device in neighbours:
+        pl.semaphore_signal(barrier, inc=1, device_id=device, device_id_type=MESH)
+
+
+    def load_rest():
+        load_weight(0)
+        for w in range(1, len(KV_WAVES), 2):
+            load_hidden(w, min(w + 2, len(KV_WAVES)))
+            if len(weight_loads) < len(Y_WAVES):
+                load_weight(len(weight_loads))
+        while len(weight_loads) < len(Y_WAVES):
+            load_weight(len(weight_loads))
 
     row_i = lax.broadcasted_iota(jnp.int32, (HEAD, HEAD), 0)
     col_i = lax.broadcasted_iota(jnp.int32, (HEAD, HEAD), 1)
@@ -161,7 +165,8 @@
     waiting = {}
 
     def encode(w):
-        hidden_loads[w].wait()
+        if hidden_loads[w] is not None:
+            hidden_loads[w].wait()
 
         def tile(i, _):
             at = pl.multiple_of((KV_AT[w] + i) * 512, 512)
@@ -331,18 +336,17 @@
         waiting["pg", w].append(send(whole, whole, peer))
 
     def partial(v):
-        for copy in weight_loads[v]:
-            copy.wait()
-        tile_rows = 512
+        weight_loads[v].wait()
+        size = Y_WAVES[v]
 
         def tile(i, _):
-            rows = rows_of(8 * Y_AT[v] + i * tile_rows, tile_rows)
-            part[rows, :] = lax.dot_general(
-                weight[rows, :], masked[...], (((1,), (1,)), ((), ())), preferred_element_type=F32
+            rows = weight[pl.ds(i * 4, 4), pl.ds(Y_AT[v], size), :].reshape(4 * size, 512)
+            part[rows_of(8 * Y_AT[v] + i * 4 * size, 4 * size), :] = lax.dot_general(
+                rows, masked[...], (((1,), (1,)), ((), ())), preferred_element_type=F32
             ).astype(BF16)
             return 0
 
-        lax.fori_loop(0, 8 * Y_WAVES[v] // tile_rows, tile, 0)
+        lax.fori_loop(0, 2, tile, 0)
 
     def do_y_end(v):
         y_axis.arrive(v)
@@ -361,13 +365,15 @@
         input_out[pl.ds(Y_AT[v], half), :] = total
 
     met = False
-    for name, w in order():
+    for name, w in ORDER:
         if name == "encode":
             encode(w)
             if not met:
                 pl.semaphore_wait(barrier, len(neighbours))
+            pair_send(w)
+            if not met:
+                load_rest()
                 met = True
-            pair_send(w)
         elif name == "pair":
             do_pair(w)
         elif name == "x_mid":
@@ -416,7 +422,7 @@
         out_specs=(vmem, vmem),
         scratch_shapes=[
             pltpu.VMEM((512, 4608), BF16),
-            pltpu.VMEM((4608, 512), BF16),
+            pltpu.VMEM((8, 576, 512), BF16),
             pltpu.VMEM((512, 512), BF16),
             pltpu.VMEM((1, 512), jnp.int32),
             pltpu.VMEM((1, 256), F32),
@@ -436,18 +442,21 @@
             pltpu.VMEM((1152, 512), BF16),
             pltpu.VMEM((576, 512), BF16),
             pltpu.SemaphoreType.DMA((64,)),
-            pltpu.SemaphoreType.DMA((192,)),
-            pltpu.SemaphoreType.DMA((192,)),
+            pltpu.SemaphoreType.DMA((288,)),
+            pltpu.SemaphoreType.DMA((288,)),
         ],
         compiler_params=pltpu.CompilerParams(
             collective_id=0, has_side_effects=True, vmem_limit_bytes=48 * 2**20
         ),
         cost_estimate=pl.CostEstimate(flops=5 * 10**9, bytes_accessed=15 * 10**6, transcendentals=0),
         name="reduce_both",
-    )(
-        token_counts, hidden_in, kv_weight, kv_cotangent, block_signs.reshape(1, 512), level_table.reshape(1, 256),
-        level_index,
-    )
+    )(token_counts, *(
+        pltpu.with_memory_space_constraint(array, pltpu.HBM)
+        for array in (
+            hidden_in, kv_weight.reshape(8, 576, 512), kv_cotangent, block_signs.reshape(1, 512),
+            level_table.reshape(1, 256), level_index,
+        )
+    ))
     return input_t.T, grad
 
 

time: 88 us -> 73 us (0.83)
  Pallas kernels: 80.2 us -> 68.6 us
  local copies, waits for them, and re-layouts: 6.28 us -> 3 us
    pallas_call x1, Pallas kernels: 80.2 us -> 68.6 us  [local(): pl.pallas_call(kernel, out_shape=(jax.ShapeDtypeStruct((4608, 512), BF16)...]
    unnamed x10 -> x2, local copies, waits for them, and re-layouts: 6.28 us -> 3 us
where the time goes in v2:
time: 73 us; the launch traced here: 72.9 us
  Pallas kernels  68.6 us (94%)
  local copies, waits for them, and re-layouts  3 us (4%)
  between operations  1.29 us (2%)
    pallas_call x1, Pallas kernels, local(): pl.pallas_call(kernel, out_shape=(jax.ShapeDtypeStruct((4608, 512), BF16)...  68.6 us
    unnamed x2, local copies, waits for them, and re-layouts  3 us

profile of v2, /device:TPU:1, one launch (start us, length us, event | category | flops | bytes accessed | tf_op | source)
XLA Modules:
  0.0 72.9 jit_solution(17821477296454959477)
XLA Ops:
  1.3 68.6 %reduce_both.1 = (bf16[4608,512]{1,0:T(8,128)(2,1)S(1)}, bf16[576,512]{1,0:T(8,128)(2,1)S(1)}) custom-call(s32[1]{0:T(128)S(6)} %copy.11.count, bf16[512,4608]{1,0:T(8,128)(2,1)} %hidden_hbm.1, bf16[8,576,512]{2,1,0:T(8,128)(2,1)} %bitcast.5, bf16[512,512]{1,0:T(8,128)(2,1)} %cot_hbm.1, s32[1,512]{1,0:T(1,128)} %bitcast.6, f32[1,256]{1,0:T(1,128)} %bitcast.7, ...), custom_call_target="tpu_custom_call" | custom-call | flops 5000000000 | bytes 15000000 | tf_op jit(solution)/shard_map/reduce_both/pallas_call | solution.py:415
  69.9 0.8 %copy.12 = bf16[512,576]{0,1:T(8,128)(2,1)} copy(bf16[512,576]{0,1:T(8,128)(2,1)S(1)} %bitcast.4) | data formatting | bytes 1179648
  70.8 2.2 %copy.13 = bf16[4608,512]{1,0:T(8,128)(2,1)} copy(bf16[4608,512]{1,0:T(8,128)(2,1)S(1)} %get-tuple-element.9) | data formatting | bytes 9437184

commit v3 on v2

v3 whole, which is shorter than its diff:
```python
import functools
import math

import jax
import jax.numpy as jnp
from jax import lax
from jax.experimental import pallas as pl
from jax.experimental.pallas import tpu as pltpu
from jax.sharding import PartitionSpec as P

MESH = pl.DeviceIdType.MESH
SEND_SLOTS = 16
F32 = jnp.float32
BF16 = jnp.bfloat16
HEAD = 128
NX, NZ, NY = 4, 4, 4

KV_WAVES = (1, 1, 1, 1, 1, 1, 1, 1, 1)
Y_WAVES = (64, 128, 128, 128, 128)


def starts(sizes):
    out, at = [], 0
    for size in sizes:
        out.append(at)
        at += size
    return tuple(out)


KV_AT = starts(KV_WAVES)
Y_AT = starts(Y_WAVES)


ORDER = (
    ("encode", 0), ("partial", 0), ("encode", 1), ("encode", 2), ("pair", 0), ("encode", 3), ("pair", 1),
    ("encode", 4), ("pair", 2), ("partial", 1), ("encode", 5), ("x_mid", 0), ("encode", 6), ("pair", 4),
    ("encode", 7), ("x_mid", 1), ("x_mid", 2), ("pair", 3), ("partial", 4), ("x_end", 0), ("x_mid", 4),
    ("partial", 2), ("pair", 5), ("x_end", 1), ("encode", 8), ("x_end", 2), ("x_mid", 3), ("pair", 6),
    ("pair", 7), ("x_end", 4), ("z_end", 0), ("pair", 8), ("x_end", 3), ("x_mid", 6), ("z_end", 1),
    ("partial", 3), ("z_end", 2), ("y_mid", 0), ("x_mid", 5), ("z_end", 4), ("x_mid", 8), ("y_mid", 1),
    ("y_mid", 2), ("x_end", 6), ("x_mid", 7), ("x_own", 0), ("x_end", 5), ("x_end", 8), ("x_own", 1),
    ("x_end", 7), ("x_own", 2), ("z_end", 3), ("x_own", 4), ("z_end", 6), ("z_end", 5), ("x_pass", 2),
    ("z_end", 8), ("x_pass", 0), ("x_pass", 4), ("y_mid", 3), ("x_pass", 1), ("z_end", 7), ("y_end", 1),
    ("x_own", 3), ("y_mid", 4), ("x_own", 6), ("y_end", 2), ("x_own", 5), ("x_own", 8), ("y_end", 3),
    ("y_end", 0), ("x_own", 7), ("x_pass", 3), ("y_end", 4), ("zl_end", 1), ("pair_last", 0), ("pair_last", 2),
    ("x_pass", 5), ("x_pass", 6), ("x_pass", 8), ("pair_last", 4), ("pair_last", 1), ("x_pass", 7),
    ("pair_last", 3), ("pair_last", 5), ("pair_last", 6), ("pair_last", 8), ("zl_end", 3), ("pair_last", 7),
    ("zl_end", 0), ("zl_end", 2), ("zl_end", 4),
)


def rows_of(at, size):
    return pl.ds(pl.multiple_of(at, 16), size)


def add_rows(out, out_at, terms, size, block=32):
    block = min(block, size)

    def step(i, _):
        total = None
        for ref, at in terms:
            value = ref[rows_of(at + i * block, block), :].astype(F32)
            total = value if total is None else total + value
        out[rows_of(out_at + i * block, block), :] = total.astype(BF16)
        return 0

    lax.fori_loop(0, size // block, step, 0)


def kernel(
    count, hidden_hbm, weight_hbm, cot_hbm, signs_hbm, table_hbm, index_hbm,
    grad_out, input_out,
    hidden, weight, masked, signs, table, index, bt, enc, pair_in, summed,
    x_mid_in, x_in, x_sum, z_in, part, y_mid_in, y_in, y_sum, zl_in,
    local_sem, send_sem, recv_sem,
):
    dp, tensor = lax.axis_index("dp"), lax.axis_index("tensor")
    zh, x, core = dp // 8, (dp // 2) % 4, dp % 2
    y, zl = tensor // 2, tensor % 2

    def dp_of(zh_, x_, core_):
        return ((zh_ % 4) * 4 + (x_ % 4)) * 2 + core_

    def at_dp(zh_, x_, core_):
        return (dp_of(zh_, x_, core_), tensor)

    peer = at_dp(zh, x, 1 - core)
    x_next, x_prev = at_dp(zh, x + 1, core), at_dp(zh, x + 3, core)
    z_next, z_prev, z_far = at_dp(zh + 1, x, core), at_dp(zh + 3, x, core), at_dp(zh + 2, x, core)
    z_others = ((zh + 1, z_next), (zh + 3, z_prev), (zh + 2, z_far))
    y_next, y_prev = (dp, ((y + 1) % 4) * 2 + zl), (dp, ((y + 3) % 4) * 2 + zl)
    zl_peer = (dp, y * 2 + 1 - zl)
    neighbours = (peer, x_next, x_prev, z_next, z_prev, z_far, y_next, y_prev, zl_peer)

    local_used = [0]
    arrivals = {}
    slots = [0] * SEND_SLOTS
    slot = [0]

    def drain(semaphore, rows):
        view = enc.at[pl.ds(0, rows), :]
        pltpu.make_async_copy(view, view, semaphore).wait()

    def wait_for(key):
        index, rows = arrivals.pop(key)
        drain(recv_sem.at[index], rows)

    recv_of = {}

    def next_slot():
        slot[0] = (slot[0] + 1) % SEND_SLOTS
        if slots[slot[0]]:
            drain(send_sem.at[slot[0]], slots[slot[0]])
            slots[slot[0]] = 0

    def load(src, dst):
        copy = pltpu.make_async_copy(src, dst, local_sem.at[local_used[0]])
        local_used[0] += 1
        copy.start()
        return copy

    def send(src, dst, device, key):
        index = recv_of.setdefault(key, len(recv_of))
        rows = src.shape[0] * src.shape[1] // 512
        copy = pltpu.make_async_remote_copy(
            src_ref=src, dst_ref=dst, send_sem=send_sem.at[slot[0]], recv_sem=recv_sem.at[index],
            device_id=device, device_id_type=MESH,
        )
        copy.start()
        slots[slot[0]] += rows
        arrivals[key] = [index, arrivals.get(key, (0, 0))[1] + rows]

    cot_load = load(cot_hbm, masked)
    barrier = pltpu.get_barrier_semaphore()
    for device in neighbours:
        pl.semaphore_signal(barrier, inc=1, device_id=device, device_id_type=MESH)
    small_loads = [load(signs_hbm, signs), load(table_hbm, table), load(index_hbm, index)]
    hidden_loads, weight_loads = [], []

    def load_hidden(first, last):
        lanes = pl.ds(KV_AT[first] * 512, sum(KV_WAVES[first:last]) * 512)
        copy = load(hidden_hbm.at[:, lanes], hidden.at[:, lanes])
        hidden_loads.extend([copy] + [None] * (last - first - 1))

    def load_weight(v):
        rows = pl.ds(Y_AT[v], Y_WAVES[v])
        weight_loads.append(load(weight_hbm.at[:, rows, :], weight.at[:, rows, :]))

    load_hidden(0, 1)
    def load_rest():
        load_weight(0)
        for w in range(1, len(KV_WAVES), 2):
            load_hidden(w, min(w + 2, len(KV_WAVES)))
            if len(weight_loads) < len(Y_WAVES):
                load_weight(len(weight_loads))
        while len(weight_loads) < len(Y_WAVES):
            load_weight(len(weight_loads))

    row_i = lax.broadcasted_iota(jnp.int32, (HEAD, HEAD), 0)
    col_i = lax.broadcasted_iota(jnp.int32, (HEAD, HEAD), 1)
    common = row_i & col_i
    common = common ^ (common >> 4)
    common = common ^ (common >> 2)
    common = common ^ (common >> 1)
    hadamard = (1 - 2 * (common & 1)).astype(F32)

    cot_load.wait()
    tokens = lax.broadcasted_iota(jnp.int32, (512, 512), 0)
    masked[...] = jnp.where(tokens < count[0], masked[...].astype(F32), 0.0).astype(BF16)
    for copy in small_loads:
        copy.wait()
    sign_row = (2 * signs[...] - 1).astype(F32)
    for j in range(4):
        lanes = pl.ds(j * HEAD, HEAD)
        turned = (hadamard * sign_row[:, j * HEAD:(j + 1) * HEAD]).astype(BF16)
        bt[lanes, :] = (
            lax.dot_general(turned, masked[:, lanes], (((1,), (1,)), ((), ())), preferred_element_type=F32)
            * (1.0 / 256.0)
        ).astype(BF16)

    def encode(w):
        if hidden_loads[w] is not None:
            hidden_loads[w].wait()

        def tile(i, _):
            at = pl.multiple_of((KV_AT[w] + i) * 512, 512)
            value = jnp.dot(bt[...], hidden[:, pl.ds(at, 512)], preferred_element_type=F32)
            low = jnp.broadcast_to(table[:, 0:128], (4, 128))
            high = jnp.broadcast_to(table[:, 128:256], (4, 128))
            bounds = []
            for k in range(4):
                ids = index[:, pl.ds(at + k * 128, 128)]
                first = jnp.take_along_axis(low, ids & 127, axis=1, mode="promise_in_bounds")
                second = jnp.take_along_axis(high, ids & 127, axis=1, mode="promise_in_bounds")
                bounds.append(jnp.where(ids >= 128, second, first))
            bound = jnp.concatenate(bounds, axis=1)
            for j in range(4):
                limit = bound[j:j + 1, :]
                clipped = jnp.clip(value[j * HEAD:(j + 1) * HEAD], -limit, limit).astype(BF16)
                enc[pl.ds(at, 512), pl.ds(j * HEAD, HEAD)] = clipped.T
            return 0

        lax.fori_loop(0, KV_WAVES[w], tile, 0)

    def own_rows(w, core_):
        g = KV_WAVES[w]
        return KV_AT[w] * 512 + core_ * 256 * g, 256 * g

    def pair_send(w):
        at, size = own_rows(w, 1 - core)
        send(enc.at[rows_of(at, size), :], pair_in.at[pl.ds(KV_AT[w] * 256, size), :], peer, ("pair", w))

    class Axis:
        def __init__(self, name, place, following, previous, source, mid_in, into):
            self.name, self.place, self.next, self.prev = name, place, following, previous
            self.source, self.mid_in, self.into = source, mid_in, into

        def piece(self, ref, base, chunk, half, h):
            return ref.at[rows_of(base + chunk * 2 * half + h * half, half), :]

        def begin(self, w, base, half, at):
            mid_rows = pl.ds(at // 2, half)
            here = functools.partial(self.piece, self.source, base)
            far, up, down = (self.place + 2) % 4, (self.place + 1) % 4, (self.place + 3) % 4
            send(here(far, half, 0), self.mid_in.at[0, mid_rows], self.next, (self.name, "mid", w))
            send(here(far, half, 1), self.mid_in.at[1, mid_rows], self.prev, (self.name, "mid", w))
            send(here(up, half, 1), self.piece(self.into.at[0], at, 0, half, 1), self.next, (self.name, "end", w))
            send(here(down, half, 0), self.piece(self.into.at[1], at, 0, half, 0), self.prev, (self.name, "end", w))

        def middle(self, w, base, half, at):
            up, down = (self.place + 1) % 4, (self.place + 3) % 4
            wait_for((self.name, "mid", w))
            for h, chunk, device in ((0, up, self.next), (1, down, self.prev)):
                first = base + chunk * 2 * half + h * half
                add_rows(self.source, first, ((self.source, first), (self.mid_in.at[h], at // 2)), half)
                send(
                    self.piece(self.source, base, chunk, half, h), self.piece(self.into.at[h], at, 0, half, h), device,
                    (self.name, "end", w),
                )

        def arrive(self, w):
            wait_for((self.name, "end", w))

    x_axis = Axis("x", x, x_next, x_prev, summed, x_mid_in, x_in)
    y_axis = Axis("y", y, y_next, y_prev, part, y_mid_in, y_in)

    def x_args(w):
        g = KV_WAVES[w]
        return KV_AT[w] * 256, 32 * g, KV_AT[w] * 64

    def z_args(w):
        g = KV_WAVES[w]
        return KV_AT[w] * 64, 16 * g

    def y_args(v):
        return 8 * Y_AT[v], Y_WAVES[v], 2 * Y_AT[v]

    def chunk_row(w, x_, zh_=None):
        g = KV_WAVES[w]
        row = KV_AT[w] * 512 + core * 256 * g + (x_ % 4) * 64 * g
        return row if zh_ is None else row + (zh_ % 4) * 16 * g

    def do_pair(w):
        wait_for(("pair", w))
        at, size = own_rows(w, core)
        add_rows(summed, KV_AT[w] * 256, ((enc, at), (pair_in, KV_AT[w] * 256)), size)
        x_axis.begin(w, *x_args(w))

    def do_x_end(w):
        x_axis.arrive(w)
        base, half, at = x_args(w)
        add_rows(
            x_sum, at, ((summed, base + x * 2 * half), (x_in.at[0], at), (x_in.at[1], at)), 2 * half
        )
        base, size = z_args(w)
        for i, (place, device) in enumerate(z_others):
            send(
                x_sum.at[rows_of(base + (place % 4) * size, size), :], z_in.at[i, pl.ds(KV_AT[w] * 16, size), :], device,
                ("z_end", w),
            )

    def do_z_end(w):
        wait_for(("z_end", w))
        base, half = z_args(w)
        rows = pl.ds(KV_AT[w] * 16, half)
        total = x_sum[rows_of(base + zh * half, half), :].astype(F32)
        for i in range(3):
            total = total + z_in[i, rows].astype(F32)
        requant = (total * (1.0 / math.sqrt(32.0))).astype(BF16)
        row = chunk_row(w, x, zh)
        for j in range(4):
            lanes = slice(j * HEAD, (j + 1) * HEAD)
            decoded = jnp.dot(requant[:, lanes], hadamard.astype(BF16), preferred_element_type=F32)
            grad_out[rows_of(row, half), lanes] = (
                decoded * (1.0 / math.sqrt(HEAD)) * sign_row[:, lanes]
            ).astype(BF16)
        whole = grad_out.at[rows_of(row, half), :]
        for _, device in z_others:
            send(whole, whole, device, ("z_own", w))

    def do_x_own(w):
        wait_for(("z_own", w))
        whole = grad_out.at[rows_of(chunk_row(w, x), 64 * KV_WAVES[w]), :]
        send(whole, whole, x_next, ("x_own", w))
        send(whole, whole, x_prev, ("x_own", w))
        send(whole, whole, peer, "last")

    def do_x_pass(w):
        half = 32 * KV_WAVES[w]
        wait_for(("x_own", w))
        for place, device, first in ((x + 3, x_next, 0), (x + 1, x_prev, half)):
            piece = grad_out.at[rows_of(chunk_row(w, place) + first, half), :]
            send(piece, piece, device, ("x_pass", w))
        for place in (x + 3, x + 1):
            whole = grad_out.at[rows_of(chunk_row(w, place), 2 * half), :]
            send(whole, whole, peer, "last")

    def do_pair_last(w):
        wait_for(("x_pass", w))
        whole = grad_out.at[rows_of(chunk_row(w, x + 2), 64 * KV_WAVES[w]), :]
        send(whole, whole, peer, "last")

    def partial(v):
        weight_loads[v].wait()
        size = Y_WAVES[v]

        def tile(i, _):
            rows = weight[pl.ds(i * 4, 4), pl.ds(Y_AT[v], size), :].reshape(4 * size, 512)
            part[rows_of(8 * Y_AT[v] + i * 4 * size, 4 * size), :] = lax.dot_general(
                rows, masked[...], (((1,), (1,)), ((), ())), preferred_element_type=F32
            ).astype(BF16)
            return 0

        lax.fori_loop(0, 2, tile, 0)

    def do_y_end(v):
        y_axis.arrive(v)
        base, half, at = y_args(v)
        add_rows(y_sum, at, ((part, base + y * 2 * half), (y_in.at[0], at), (y_in.at[1], at)), 2 * half)
        send(y_sum.at[rows_of(at + (1 - zl) * half, half), :], zl_in.at[pl.ds(Y_AT[v], half), :], zl_peer, ("zl", v))

    def do_zl_end(v):
        wait_for(("zl", v))
        base, half, at = y_args(v)
        total = (
            y_sum[rows_of(at + zl * half, half), :].astype(F32) + zl_in[pl.ds(Y_AT[v], half), :].astype(F32)
        ).astype(BF16)
        input_out[pl.ds(Y_AT[v], half), :] = total

    met = False
    for name, w in ORDER:
        next_slot()
        if name == "encode":
            encode(w)
            if not met:
                pl.semaphore_wait(barrier, len(neighbours))
            pair_send(w)
            if not met:
                load_rest()
                met = True
        elif name == "pair":
            do_pair(w)
        elif name == "x_mid":
            x_axis.middle(w, *x_args(w))
        elif name == "x_end":
            do_x_end(w)
        elif name == "z_end":
            do_z_end(w)
        elif name == "x_own":
            do_x_own(w)
        elif name == "x_pass":
            do_x_pass(w)
        elif name == "pair_last":
            do_pair_last(w)
        elif name == "partial":
            partial(w)
            y_axis.begin(w, *y_args(w))
        elif name == "y_mid":
            y_axis.middle(w, *y_args(w))
        elif name == "y_end":
            do_y_end(w)
        elif name == "zl_end":
            do_zl_end(w)

    wait_for("last")
    for index, rows in enumerate(slots):
        if rows:
            drain(send_sem.at[index], rows)


def local(hidden_in, kv_weight, kv_cotangent, token_counts, block_signs, level_table, level_index):
    hbm = pl.BlockSpec(memory_space=pltpu.HBM)
    vmem = pl.BlockSpec(memory_space=pltpu.VMEM)
    grad, input_t = pl.pallas_call(
        kernel,
        out_shape=(
            jax.ShapeDtypeStruct((4608, 512), BF16),
            jax.ShapeDtypeStruct((576, 512), BF16),
        ),
        in_specs=[pl.BlockSpec(memory_space=pltpu.SMEM)] + [hbm] * 6,
        out_specs=(vmem, vmem),
        scratch_shapes=[
            pltpu.VMEM((512, 4608), BF16),
            pltpu.VMEM((8, 576, 512), BF16),
            pltpu.VMEM((512, 512), BF16),
            pltpu.VMEM((1, 512), jnp.int32),
            pltpu.VMEM((1, 256), F32),
            pltpu.VMEM((4, 4608), jnp.int32),
            pltpu.VMEM((512, 512), BF16),
            pltpu.VMEM((4608, 512), BF16),
            pltpu.VMEM((2304, 512), BF16),
            pltpu.VMEM((2304, 512), BF16),
            pltpu.VMEM((2, 288, 512), BF16),
            pltpu.VMEM((2, 576, 512), BF16),
            pltpu.VMEM((576, 512), BF16),
            pltpu.VMEM((3, 144, 512), BF16),
            pltpu.VMEM((4608, 512), BF16),
            pltpu.VMEM((2, 576, 512), BF16),
            pltpu.VMEM((2, 1152, 512), BF16),
            pltpu.VMEM((1152, 512), BF16),
            pltpu.VMEM((576, 512), BF16),
            pltpu.SemaphoreType.DMA((14,)),
            pltpu.SemaphoreType.DMA((SEND_SLOTS,)),
            pltpu.SemaphoreType.DMA((7 * len(KV_WAVES) + 3 * len(Y_WAVES) + 1,)),
        ],
        compiler_params=pltpu.CompilerParams(
            collective_id=0, has_side_effects=True, vmem_limit_bytes=48 * 2**20
        ),
        cost_estimate=pl.CostEstimate(flops=5 * 10**9, bytes_accessed=15 * 10**6, transcendentals=0),
        name="reduce_both",
    )(token_counts, *(
        pltpu.with_memory_space_constraint(array, pltpu.HBM)
        for array in (
            hidden_in, kv_weight.reshape(8, 576, 512), kv_cotangent, block_signs.reshape(1, 512),
            level_table.reshape(1, 256), level_index,
        )
    ))
    return input_t.T, grad


def solution(mesh):
    return jax.shard_map(
        local,
        mesh=mesh,
        in_specs=(
            P("dp", None),
            P(None, "tensor"),
            P("dp", "tensor"),
            P("dp"),
            P("tensor"),
            P(),
            P("tensor", None),
        ),
        out_specs=(P("dp", "tensor"), P(None, "tensor")),
        check_vma=False,
    )
```

time: 73 us -> 66.4 us (0.910)
  Pallas kernels: 68.6 us -> 62 us
    pallas_call x1, Pallas kernels: 68.6 us -> 62 us  [local(): pl.pallas_call(kernel, out_shape=(jax.ShapeDtypeStruct((4608, 512), BF16)...]
where the time goes in v3:
time: 66.4 us; the launch traced here: 66.3 us
  Pallas kernels  62 us (93%)
  local copies, waits for them, and re-layouts  3 us (5%)
  between operations  1.29 us (2%)
    pallas_call x1, Pallas kernels, local(): pl.pallas_call(kernel, out_shape=(jax.ShapeDtypeStruct((4608, 512), BF16)...  62 us
    unnamed x2, local copies, waits for them, and re-layouts  3 us

profile of v3, /device:TPU:1, one launch (start us, length us, event | category | flops | bytes accessed | tf_op | source)
XLA Modules:
  0.0 66.3 jit_solution(14229532406911696922)
XLA Ops:
  1.3 62.0 %reduce_both.1 = (bf16[4608,512]{1,0:T(8,128)(2,1)S(1)}, bf16[576,512]{1,0:T(8,128)(2,1)S(1)}) custom-call(s32[1]{0:T(128)S(6)} %copy.11.count, bf16[512,4608]{1,0:T(8,128)(2,1)} %hidden_hbm.1, bf16[8,576,512]{2,1,0:T(8,128)(2,1)} %bitcast.5, bf16[512,512]{1,0:T(8,128)(2,1)} %cot_hbm.1, s32[1,512]{1,0:T(1,128)} %bitcast.6, f32[1,256]{1,0:T(1,128)} %bitcast.7, ...), custom_call_target="tpu_custom_call" | custom-call | flops 5000000000 | bytes 15000000 | tf_op jit(solution)/shard_map/reduce_both/pallas_call | solution.py:394
  63.3 0.8 %copy.12 = bf16[512,576]{0,1:T(8,128)(2,1)} copy(bf16[512,576]{0,1:T(8,128)(2,1)S(1)} %bitcast.4) | data formatting | bytes 1179648
  64.1 2.2 %copy.13 = bf16[4608,512]{1,0:T(8,128)(2,1)} copy(bf16[4608,512]{1,0:T(8,128)(2,1)S(1)} %get-tuple-element.9) | data formatting | bytes 9437184

commit v4 on v3

--- a/solution.py
+++ b/solution.py
@@ -16,7 +16,10 @@
 NX, NZ, NY = 4, 4, 4
 
 KV_WAVES = (1, 1, 1, 1, 1, 1, 1, 1, 1)
-Y_WAVES = (64, 128, 128, 128, 128)
+Y_WAVES = (64, 64, 64, 64, 64, 64, 64, 64, 64)
+
+
+Z_DIRECT = (True, True, True, True, True, True, True, True, True)
 
 
 def starts(sizes):
@@ -32,20 +35,22 @@
 
 
 ORDER = (
-    ("encode", 0), ("partial", 0), ("encode", 1), ("encode", 2), ("pair", 0), ("encode", 3), ("pair", 1),
-    ("encode", 4), ("pair", 2), ("partial", 1), ("encode", 5), ("x_mid", 0), ("encode", 6), ("pair", 4),
-    ("encode", 7), ("x_mid", 1), ("x_mid", 2), ("pair", 3), ("partial", 4), ("x_end", 0), ("x_mid", 4),
-    ("partial", 2), ("pair", 5), ("x_end", 1), ("encode", 8), ("x_end", 2), ("x_mid", 3), ("pair", 6),
-    ("pair", 7), ("x_end", 4), ("z_end", 0), ("pair", 8), ("x_end", 3), ("x_mid", 6), ("z_end", 1),
-    ("partial", 3), ("z_end", 2), ("y_mid", 0), ("x_mid", 5), ("z_end", 4), ("x_mid", 8), ("y_mid", 1),
-    ("y_mid", 2), ("x_end", 6), ("x_mid", 7), ("x_own", 0), ("x_end", 5), ("x_end", 8), ("x_own", 1),
-    ("x_end", 7), ("x_own", 2), ("z_end", 3), ("x_own", 4), ("z_end", 6), ("z_end", 5), ("x_pass", 2),
-    ("z_end", 8), ("x_pass", 0), ("x_pass", 4), ("y_mid", 3), ("x_pass", 1), ("z_end", 7), ("y_end", 1),
-    ("x_own", 3), ("y_mid", 4), ("x_own", 6), ("y_end", 2), ("x_own", 5), ("x_own", 8), ("y_end", 3),
-    ("y_end", 0), ("x_own", 7), ("x_pass", 3), ("y_end", 4), ("zl_end", 1), ("pair_last", 0), ("pair_last", 2),
-    ("x_pass", 5), ("x_pass", 6), ("x_pass", 8), ("pair_last", 4), ("pair_last", 1), ("x_pass", 7),
-    ("pair_last", 3), ("pair_last", 5), ("pair_last", 6), ("pair_last", 8), ("zl_end", 3), ("pair_last", 7),
-    ("zl_end", 0), ("zl_end", 2), ("zl_end", 4),
+    ("encode", 0), ("partial", 0), ("encode", 1), ("pair", 0), ("encode", 2), ("partial", 2), ("encode", 3),
+    ("pair", 1), ("encode", 4), ("encode", 5), ("x_mid", 0), ("partial", 3), ("pair", 3), ("partial", 5),
+    ("encode", 6), ("x_mid", 1), ("pair", 4), ("x_end", 0), ("x_mid", 3), ("pair", 2), ("encode", 7),
+    ("y_mid", 2), ("encode", 8), ("x_end", 1), ("x_mid", 4), ("pair", 6), ("partial", 8), ("x_end", 3),
+    ("y_mid", 5), ("x_mid", 2), ("z_end", 0), ("pair", 5), ("pair", 8), ("x_end", 4), ("x_mid", 6),
+    ("partial", 4), ("x_end", 2), ("pair", 7), ("z_end", 1), ("partial", 6), ("x_mid", 8), ("z_end", 3),
+    ("x_mid", 5), ("x_end", 6), ("partial", 1), ("x_mid", 7), ("z_end", 4), ("x_own", 0), ("x_end", 8),
+    ("y_mid", 0), ("x_own", 1), ("x_end", 5), ("y_mid", 1), ("x_own", 3), ("x_end", 7), ("y_mid", 8),
+    ("z_end", 2), ("partial", 7), ("y_mid", 6), ("y_mid", 4), ("x_pass", 1), ("x_pass", 0), ("x_own", 4),
+    ("z_end", 6), ("z_end", 8), ("y_mid", 3), ("z_end", 5), ("x_pass", 3), ("z_end", 7), ("x_own", 2),
+    ("x_pass", 4), ("y_end", 0), ("x_own", 6), ("y_mid", 7), ("x_own", 8), ("y_end", 8), ("y_end", 1),
+    ("y_end", 6), ("x_own", 5), ("y_end", 3), ("x_own", 7), ("y_end", 2), ("y_end", 5), ("y_end", 4),
+    ("x_pass", 6), ("x_pass", 8), ("pair_last", 3), ("pair_last", 0), ("x_pass", 2), ("zl_end", 1),
+    ("x_pass", 5), ("pair_last", 4), ("pair_last", 1), ("zl_end", 0), ("x_pass", 7), ("y_end", 7),
+    ("pair_last", 2), ("pair_last", 6), ("zl_end", 2), ("pair_last", 8), ("pair_last", 5), ("pair_last", 7),
+    ("zl_end", 6), ("zl_end", 3), ("zl_end", 8), ("zl_end", 4), ("zl_end", 5), ("zl_end", 7),
 )
 
 
@@ -131,11 +136,13 @@
         arrivals[key] = [index, arrivals.get(key, (0, 0))[1] + rows]
 
     cot_load = load(cot_hbm, masked)
+    lanes = pl.ds(0, KV_WAVES[0] * 512)
+    hidden_loads = [load(hidden_hbm.at[:, lanes], hidden.at[:, lanes])]
     barrier = pltpu.get_barrier_semaphore()
     for device in neighbours:
         pl.semaphore_signal(barrier, inc=1, device_id=device, device_id_type=MESH)
     small_loads = [load(signs_hbm, signs), load(table_hbm, table), load(index_hbm, index)]
-    hidden_loads, weight_loads = [], []
+    weight_loads = []
 
     def load_hidden(first, last):
         lanes = pl.ds(KV_AT[first] * 512, sum(KV_WAVES[first:last]) * 512)
@@ -146,9 +153,8 @@
         rows = pl.ds(Y_AT[v], Y_WAVES[v])
         weight_loads.append(load(weight_hbm.at[:, rows, :], weight.at[:, rows, :]))
 
-    load_hidden(0, 1)
+    load_weight(0)
     def load_rest():
-        load_weight(0)
         for w in range(1, len(KV_WAVES), 2):
             load_hidden(w, min(w + 2, len(KV_WAVES)))
             if len(weight_loads) < len(Y_WAVES):
@@ -295,8 +301,19 @@
                 decoded * (1.0 / math.sqrt(HEAD)) * sign_row[:, lanes]
             ).astype(BF16)
         whole = grad_out.at[rows_of(row, half), :]
-        for _, device in z_others:
-            send(whole, whole, device, ("z_own", w))
+        if Z_DIRECT[w]:
+            for _, device in z_others:
+                send(whole, whole, device, ("z_own", w))
+        else:
+            for _, device in z_others[:2]:
+                send(whole, whole, device, ("z_first", w))
+
+    def do_z_pass(w):
+        half = 16 * KV_WAVES[w]
+        wait_for(("z_first", w))
+        for place, device, lanes in ((zh + 3, z_next, pl.ds(0, 256)), (zh + 1, z_prev, pl.ds(256, 256))):
+            piece = grad_out.at[rows_of(chunk_row(w, x, place), half), lanes]
+            send(piece, piece, device, ("z_own", w))
 
     def do_x_own(w):
         wait_for(("z_own", w))
@@ -347,17 +364,15 @@
         ).astype(BF16)
         input_out[pl.ds(Y_AT[v], half), :] = total
 
-    met = False
+    encode(0)
+    partial(0)
+    pl.semaphore_wait(barrier, len(neighbours))
     for name, w in ORDER:
         next_slot()
         if name == "encode":
-            encode(w)
-            if not met:
-                pl.semaphore_wait(barrier, len(neighbours))
+            if w > 0:
+                encode(w)
             pair_send(w)
-            if not met:
-                load_rest()
-                met = True
         elif name == "pair":
             do_pair(w)
         elif name == "x_mid":
@@ -366,6 +381,8 @@
             do_x_end(w)
         elif name == "z_end":
             do_z_end(w)
+        elif name == "z_pass":
+            do_z_pass(w)
         elif name == "x_own":
             do_x_own(w)
         elif name == "x_pass":
@@ -373,8 +390,11 @@
         elif name == "pair_last":
             do_pair_last(w)
         elif name == "partial":
-            partial(w)
+            if w > 0:
+                partial(w)
             y_axis.begin(w, *y_args(w))
+            if w == 0:
+                load_rest()
         elif name == "y_mid":
             y_axis.middle(w, *y_args(w))
         elif name == "y_end":
@@ -386,6 +406,17 @@
     for index, rows in enumerate(slots):
         if rows:
             drain(send_sem.at[index], rows)
+
+
+def copy_out(grad, input_t, grad_out, input_out, sem):
+    copies = [pltpu.make_async_copy(input_t, input_out, sem.at[0])]
+    for i in range(8):
+        rows = pl.ds(i * 576, 576)
+        copies.append(pltpu.make_async_copy(grad.at[rows, :], grad_out.at[rows, :], sem.at[i + 1]))
+    for copy in copies:
+        copy.start()
+    for copy in copies:
+        copy.wait()
 
 
 def local(hidden_in, kv_weight, kv_cotangent, token_counts, block_signs, level_table, level_index):
@@ -419,9 +450,9 @@
             pltpu.VMEM((2, 1152, 512), BF16),
             pltpu.VMEM((1152, 512), BF16),
             pltpu.VMEM((576, 512), BF16),
-            pltpu.SemaphoreType.DMA((14,)),
+            pltpu.SemaphoreType.DMA((9 + len(Y_WAVES),)),
             pltpu.SemaphoreType.DMA((SEND_SLOTS,)),
-            pltpu.SemaphoreType.DMA((7 * len(KV_WAVES) + 3 * len(Y_WAVES) + 1,)),
+            pltpu.SemaphoreType.DMA((7 * len(KV_WAVES) + Z_DIRECT.count(False) + 3 * len(Y_WAVES) + 1,)),
         ],
         compiler_params=pltpu.CompilerParams(
             collective_id=0, has_side_effects=True, vmem_limit_bytes=48 * 2**20
@@ -435,6 +466,15 @@
             level_table.reshape(1, 256), level_index,
         )
     ))
+    grad, input_t = pl.pallas_call(
+        copy_out,
+        out_shape=(jax.ShapeDtypeStruct((4608, 512), BF16), jax.ShapeDtypeStruct((576, 512), BF16)),
+        in_specs=[pl.BlockSpec(memory_space=pl.ANY)] * 2,
+        out_specs=(hbm, hbm),
+        scratch_shapes=[pltpu.SemaphoreType.DMA((9,))],
+        compiler_params=pltpu.CompilerParams(vmem_limit_bytes=2**20),
+        name="copy_out",
+    )(pltpu.with_memory_space_constraint(grad, pltpu.VMEM), pltpu.with_memory_space_constraint(input_t, pltpu.VMEM))
     return input_t.T, grad
 
 

time: 66.4 us -> 64.1 us (0.965)
  local copies, waits for them, and re-layouts: 3 us -> 0 us
  Pallas kernels: 62 us -> 62.7 us
    unnamed x2 -> x0, local copies, waits for them, and re-layouts: 3 us -> none
    pallas_call x0 -> x1, Pallas kernels: none -> 2.45 us  [local(): pl.pallas_call(copy_out, out_shape=(jax.ShapeDtypeStruct((4608, 512), BF1...]
    pallas_call x1, Pallas kernels: 62 us -> 60.3 us  [local(): pl.pallas_call(kernel, out_shape=(jax.ShapeDtypeStruct((4608, 512), BF16)...]
where the time goes in v4:
time: 64.1 us; the launch traced here: 64 us
  Pallas kernels  62.7 us (98%)
  between operations  1.28 us (2%)
    pallas_call x1, Pallas kernels, local(): pl.pallas_call(kernel, out_shape=(jax.ShapeDtypeStruct((4608, 512), BF16)...  60.3 us
    pallas_call x1, Pallas kernels, local(): pl.pallas_call(copy_out, out_shape=(jax.ShapeDtypeStruct((4608, 512), BF1...  2.45 us

profile of v4, /device:TPU:1, one launch (start us, length us, event | category | flops | bytes accessed | tf_op | source)
XLA Modules:
  0.0 64.0 jit_solution(4974163675913745821)
XLA Ops:
  1.3 60.3 %reduce_both.1 = (bf16[4608,512]{1,0:T(8,128)(2,1)S(1)}, bf16[576,512]{1,0:T(8,128)(2,1)S(1)}) custom-call(s32[1]{0:T(128)S(6)} %copy.9.count, bf16[512,4608]{1,0:T(8,128)(2,1)} %hidden_hbm.1, bf16[8,576,512]{2,1,0:T(8,128)(2,1)} %bitcast.4, bf16[512,512]{1,0:T(8,128)(2,1)} %cot_hbm.1, s32[1,512]{1,0:T(1,128)} %bitcast.6, f32[1,256]{1,0:T(1,128)} %bitcast.7, ...), custom_call_target="tpu_custom_call" | custom-call | flops 5000000000 | bytes 15000000 | tf_op jit(solution)/shard_map/reduce_both/pallas_call | solution.py:425
  61.6 2.4 %copy_out.1 = (bf16[4608,512]{1,0:T(8,128)(2,1)}, bf16[576,512]{1,0:T(8,128)(2,1)}) custom-call(bf16[4608,512]{1,0:T(8,128)(2,1)S(1)} %get-tuple-element.6.grad, bf16[576,512]{1,0:T(8,128)(2,1)S(1)} %get-tuple-element.7.input_t), custom_call_target="tpu_custom_call" | custom-call | tf_op jit(solution)/shard_map/copy_out/pallas_call | solution.py:469

commit v5 on v4

--- a/solution.py
+++ b/solution.py
@@ -16,10 +16,11 @@
 NX, NZ, NY = 4, 4, 4
 
 KV_WAVES = (1, 1, 1, 1, 1, 1, 1, 1, 1)
-Y_WAVES = (64, 64, 64, 64, 64, 64, 64, 64, 64)
-
-
-Z_DIRECT = (True, True, True, True, True, True, True, True, True)
+Y_WAVES = (64, 64, 64, 64, 64, 64, 64, 64, 32, 32)
+
+
+Z_DIRECT = (False, False, True, True, True, True, True, True, True)
+X_DIRECT = (False, False, False, False, False, False, False, False, False)
 
 
 def starts(sizes):
@@ -35,22 +36,23 @@
 
 
 ORDER = (
-    ("encode", 0), ("partial", 0), ("encode", 1), ("pair", 0), ("encode", 2), ("partial", 2), ("encode", 3),
-    ("pair", 1), ("encode", 4), ("encode", 5), ("x_mid", 0), ("partial", 3), ("pair", 3), ("partial", 5),
-    ("encode", 6), ("x_mid", 1), ("pair", 4), ("x_end", 0), ("x_mid", 3), ("pair", 2), ("encode", 7),
-    ("y_mid", 2), ("encode", 8), ("x_end", 1), ("x_mid", 4), ("pair", 6), ("partial", 8), ("x_end", 3),
-    ("y_mid", 5), ("x_mid", 2), ("z_end", 0), ("pair", 5), ("pair", 8), ("x_end", 4), ("x_mid", 6),
-    ("partial", 4), ("x_end", 2), ("pair", 7), ("z_end", 1), ("partial", 6), ("x_mid", 8), ("z_end", 3),
-    ("x_mid", 5), ("x_end", 6), ("partial", 1), ("x_mid", 7), ("z_end", 4), ("x_own", 0), ("x_end", 8),
-    ("y_mid", 0), ("x_own", 1), ("x_end", 5), ("y_mid", 1), ("x_own", 3), ("x_end", 7), ("y_mid", 8),
-    ("z_end", 2), ("partial", 7), ("y_mid", 6), ("y_mid", 4), ("x_pass", 1), ("x_pass", 0), ("x_own", 4),
-    ("z_end", 6), ("z_end", 8), ("y_mid", 3), ("z_end", 5), ("x_pass", 3), ("z_end", 7), ("x_own", 2),
-    ("x_pass", 4), ("y_end", 0), ("x_own", 6), ("y_mid", 7), ("x_own", 8), ("y_end", 8), ("y_end", 1),
-    ("y_end", 6), ("x_own", 5), ("y_end", 3), ("x_own", 7), ("y_end", 2), ("y_end", 5), ("y_end", 4),
-    ("x_pass", 6), ("x_pass", 8), ("pair_last", 3), ("pair_last", 0), ("x_pass", 2), ("zl_end", 1),
-    ("x_pass", 5), ("pair_last", 4), ("pair_last", 1), ("zl_end", 0), ("x_pass", 7), ("y_end", 7),
-    ("pair_last", 2), ("pair_last", 6), ("zl_end", 2), ("pair_last", 8), ("pair_last", 5), ("pair_last", 7),
-    ("zl_end", 6), ("zl_end", 3), ("zl_end", 8), ("zl_end", 4), ("zl_end", 5), ("zl_end", 7),
+    ("encode", 0), ("partial", 0), ("encode", 1), ("pair", 0), ("encode", 2), ("encode", 3), ("pair", 1),
+    ("partial", 4), ("partial", 1), ("pair", 2), ("encode", 4), ("partial", 6), ("x_mid", 0), ("pair", 3),
+    ("encode", 5), ("encode", 6), ("x_mid", 1), ("encode", 7), ("encode", 8), ("x_mid", 2), ("pair", 4),
+    ("x_end", 0), ("partial", 9), ("x_mid", 3), ("pair", 8), ("x_end", 1), ("x_end", 2), ("x_mid", 4),
+    ("partial", 5), ("x_end", 3), ("x_mid", 8), ("z_end", 0), ("pair", 5), ("pair", 6), ("x_end", 4),
+    ("pair", 7), ("z_end", 1), ("partial", 3), ("y_mid", 4), ("x_end", 8), ("z_end", 2), ("x_mid", 5),
+    ("z_pass", 0), ("x_mid", 6), ("partial", 2), ("z_end", 3), ("partial", 7), ("x_mid", 7), ("x_end", 5),
+    ("y_mid", 1), ("y_mid", 5), ("z_pass", 1), ("x_end", 6), ("x_own", 2), ("x_end", 7), ("z_end", 4),
+    ("y_mid", 9), ("x_own", 0), ("z_end", 8), ("x_own", 3), ("x_own", 1), ("z_end", 5), ("x_pass", 2),
+    ("partial", 8), ("y_mid", 6), ("x_pass", 0), ("z_end", 6), ("y_mid", 3), ("x_pass", 3), ("y_mid", 0),
+    ("z_end", 7), ("x_own", 4), ("x_pass", 1), ("y_end", 4), ("y_mid", 2), ("y_end", 1), ("y_end", 9),
+    ("pair_last", 2), ("x_own", 8), ("y_mid", 8), ("x_own", 5), ("x_own", 6), ("y_mid", 7), ("y_end", 5),
+    ("pair_last", 0), ("x_own", 7), ("y_end", 3), ("y_end", 2), ("zl_end", 4), ("x_pass", 4), ("y_end", 8),
+    ("y_end", 6), ("x_pass", 5), ("pair_last", 3), ("x_pass", 8), ("x_pass", 6), ("y_end", 7), ("x_pass", 7),
+    ("y_end", 0), ("pair_last", 1), ("zl_end", 1), ("pair_last", 5), ("zl_end", 3), ("pair_last", 4),
+    ("pair_last", 8), ("pair_last", 6), ("zl_end", 8), ("zl_end", 9), ("pair_last", 7), ("zl_end", 2),
+    ("zl_end", 7), ("zl_end", 5), ("zl_end", 6), ("zl_end", 0),
 )
 
 
@@ -91,11 +93,13 @@
 
     peer = at_dp(zh, x, 1 - core)
     x_next, x_prev = at_dp(zh, x + 1, core), at_dp(zh, x + 3, core)
+    x_far = at_dp(zh, x + 2, core)
+    x_others = ((x + 1, x_next), (x + 3, x_prev), (x + 2, x_far))
     z_next, z_prev, z_far = at_dp(zh + 1, x, core), at_dp(zh + 3, x, core), at_dp(zh + 2, x, core)
     z_others = ((zh + 1, z_next), (zh + 3, z_prev), (zh + 2, z_far))
     y_next, y_prev = (dp, ((y + 1) % 4) * 2 + zl), (dp, ((y + 3) % 4) * 2 + zl)
     zl_peer = (dp, y * 2 + 1 - zl)
-    neighbours = (peer, x_next, x_prev, z_next, z_prev, z_far, y_next, y_prev, zl_peer)
+    neighbours = (peer, x_next, x_prev, x_far, z_next, z_prev, z_far, y_next, y_prev, zl_peer)
 
     local_used = [0]
     arrivals = {}
@@ -270,14 +274,21 @@
         wait_for(("pair", w))
         at, size = own_rows(w, core)
         add_rows(summed, KV_AT[w] * 256, ((enc, at), (pair_in, KV_AT[w] * 256)), size)
-        x_axis.begin(w, *x_args(w))
+        if not X_DIRECT[w]:
+            x_axis.begin(w, *x_args(w))
+            return
+        base, half, at = x_args(w)
+        for i, (place, device) in enumerate(x_others):
+            send(
+                summed.at[rows_of(base + (place % 4) * 2 * half, 2 * half), :], x_in.at[i, pl.ds(at, 2 * half), :], device,
+                ("x", "end", w),
+            )
 
     def do_x_end(w):
         x_axis.arrive(w)
         base, half, at = x_args(w)
-        add_rows(
-            x_sum, at, ((summed, base + x * 2 * half), (x_in.at[0], at), (x_in.at[1], at)), 2 * half
-        )
+        terms = [(summed, base + x * 2 * half)] + [(x_in.at[i], at) for i in range(3 if X_DIRECT[w] else 2)]
+        add_rows(x_sum, at, terms, 2 * half)
         base, size = z_args(w)
         for i, (place, device) in enumerate(z_others):
             send(
@@ -442,7 +453,7 @@
             pltpu.VMEM((2304, 512), BF16),
             pltpu.VMEM((2304, 512), BF16),
             pltpu.VMEM((2, 288, 512), BF16),
-            pltpu.VMEM((2, 576, 512), BF16),
+            pltpu.VMEM((3, 576, 512), BF16),
             pltpu.VMEM((576, 512), BF16),
             pltpu.VMEM((3, 144, 512), BF16),
             pltpu.VMEM((4608, 512), BF16),

time: 64.1 us -> 63.3 us (0.988)
  Pallas kernels: 62.7 us -> 61.9 us
    pallas_call x1, Pallas kernels: 60.3 us -> 59.4 us  [local(): pl.pallas_call(kernel, out_shape=(jax.ShapeDtypeStruct((4608, 512), BF16)...]
where the time goes in v5:
time: 63.3 us; the launch traced here: 63.2 us
  Pallas kernels  61.9 us (98%)
  between operations  1.28 us (2%)
    pallas_call x1, Pallas kernels, local(): pl.pallas_call(kernel, out_shape=(jax.ShapeDtypeStruct((4608, 512), BF16)...  59.4 us
    pallas_call x1, Pallas kernels, local(): pl.pallas_call(copy_out, out_shape=(jax.ShapeDtypeStruct((4608, 512), BF1...  2.45 us

profile of v5, /device:TPU:1, one launch (start us, length us, event | category | flops | bytes accessed | tf_op | source)
XLA Modules:
  0.0 63.2 jit_solution(6752819487510977097)
XLA Ops:
  1.3 59.4 %reduce_both.1 = (bf16[4608,512]{1,0:T(8,128)(2,1)S(1)}, bf16[576,512]{1,0:T(8,128)(2,1)S(1)}) custom-call(s32[1]{0:T(128)S(6)} %copy.9.count, bf16[512,4608]{1,0:T(8,128)(2,1)} %hidden_hbm.1, bf16[8,576,512]{2,1,0:T(8,128)(2,1)} %bitcast.4, bf16[512,512]{1,0:T(8,128)(2,1)} %cot_hbm.1, s32[1,512]{1,0:T(1,128)} %bitcast.6, f32[1,256]{1,0:T(1,128)} %bitcast.7, ...), custom_call_target="tpu_custom_call" | custom-call | flops 5000000000 | bytes 15000000 | tf_op jit(solution)/shard_map/reduce_both/pallas_call | solution.py:436
  60.7 2.4 %copy_out.1 = (bf16[4608,512]{1,0:T(8,128)(2,1)}, bf16[576,512]{1,0:T(8,128)(2,1)}) custom-call(bf16[4608,512]{1,0:T(8,128)(2,1)S(1)} %get-tuple-element.6.grad, bf16[576,512]{1,0:T(8,128)(2,1)S(1)} %get-tuple-element.7.input_t), custom_call_target="tpu_custom_call" | custom-call | tf_op jit(solution)/shard_map/copy_out/pallas_call | solution.py:480
